TPU v7x, 32 devices: a whole 2x2x4 slice. The times are simulated.
32 devices in a mesh: job: 2 (over y), row: 4 (over z), slab: 2 (over x), pair: 2 (over core).
Axes of the slice: x: 2, y: 2, z: 4, core: 2. Of those that a mesh axis runs over, the one named last changes fastest.
Arguments:
- points: bfloat16 [32, 4096], P(None, ('job', 'row', 'slab', 'pair')), parts along dimension 1, may hold values from -5.2 to 5.2
- test_matrix: bfloat16 [256, 2048], P(None, ('row', 'slab', 'pair')), may hold values from -5 to 5
Outputs:
- sketch: float32 [4096, 256], P(('job', 'row', 'slab', 'pair')), parts along dimension 0
- core_matrix: float32 [512, 256], P('job'), parts along dimension 0
- upper_factor: float32 [512, 256], P('job'), parts along dimension 0
There are 2 independent parts, one for each index of `job`. A program takes and returns all parts, laid end to end along the dimension named above; an argument that names none is the same for every part. Nothing has to cross between parts.
All inputs are finite; a program needn't handle non-finite values.
Results may differ from a plain program's by a relative error of at most 0.0026.
Values may be sent and summed in bfloat16 or wider, within the bound.
A program may use at most 64 MiB of HBM per device.

v0:
```python
import math

import jax
import jax.numpy as jnp
from jax import lax
from jax.sharding import PartitionSpec as P


def matern_tile(row_points, col_points, length_scale):
    row_squares = jnp.sum(row_points.astype(jnp.float32) ** 2, axis=0)
    col_squares = jnp.sum(col_points.astype(jnp.float32) ** 2, axis=0)
    inner = lax.dot_general(
        row_points, col_points, (((0,), (0,)), ((), ())), preferred_element_type=jnp.float32
    )
    dist_sq = jnp.maximum(row_squares[:, None] + col_squares[None, :] - 2.0 * inner, 0.0)
    scaled = jnp.sqrt(dist_sq) / length_scale
    root_five = math.sqrt(5.0)
    values = (1.0 + root_five * scaled + 5.0 / 3.0 * scaled * scaled) * jnp.exp(-root_five * scaled)
    return values.astype(jnp.bfloat16)


def times_test(kernel_tile, test_columns):
    return lax.dot_general(
        kernel_tile, test_columns, (((1,), (1,)), ((), ())), preferred_element_type=jnp.float32
    )


def local(points, test_matrix):
    length_scale = 0.35 * math.sqrt(points.shape[0])
    block_points, block_tests = (
        lax.all_gather(points, ("slab", "pair"), axis=1, tiled=True),
        lax.all_gather(test_matrix, ("slab", "pair"), axis=1, tiled=True),
    )
    spread = lax.all_gather(points, "row", axis=1, tiled=True)
    kernel_tile = matern_tile(spread, block_points, length_scale)
    sketch = lax.psum_scatter(
        times_test(kernel_tile, block_tests), "row", scatter_dimension=0, tiled=True
    )
    total_points = (
        points.shape[1] * lax.axis_size("row") * lax.axis_size("slab") * lax.axis_size("pair")
    )
    gram_term = jnp.dot(sketch.T, sketch, precision=lax.Precision.HIGHEST)
    core_term = jnp.dot(test_matrix.astype(jnp.float32), sketch, precision=lax.Precision.HIGHEST)
    gram_sum, core_sum = lax.psum((gram_term, core_term), ("row", "slab", "pair"))
    gram = gram_sum / total_points
    core_matrix = core_sum / total_points
    upper_factor = jnp.linalg.cholesky(gram).T
    return (sketch, core_matrix, upper_factor)


def solution(mesh):
    return jax.shard_map(
        local,
        mesh=mesh,
        in_specs=(P(None, ("job", "row", "slab", "pair")), P(None, ("row", "slab", "pair"))),
        out_specs=(P(("job", "row", "slab", "pair"), None), P("job", None), P("job", None)),
        check_vma=False,
    )
```

profile of v0, /device:TPU:25, one launch (start us, length us, event | category | flops | bytes accessed | tf_op | source)
XLA Modules:
  0.0 192.0 jit_solution(8842558372499944348)
XLA Ops:
  7.2 0.0 copy-start.3
  7.2 0.0 copy-start.2
  7.2 0.0 reduce-scatter.2.cloned.1.call-start
  7.2 5.9 %all_gather.10 = bf16[32,512]{1,0:T(8,128)(2,1)S(1)} all-gather(bf16[32,128]{1,0:T(8,128)(2,1)} %param.2), channel_id=1, replica_groups=mesh['job'=2,'row'=4,'slab'=2,'pair'=2] {'slab','pair'}, dimensions={1}, use_global_device_ids=true | all-gather | bytes 40960 | tf_op jit(solution)/shard_map/all_gather | solution.py:31
  13.1 0.0 copy-done.3
  13.1 8.4 %all_gather.9 = bf16[32,512]{1,0:T(8,128)(2,1)S(1)} all-gather(bf16[32,128]{1,0:T(8,128)(2,1)S(1)} %copy-done.3), channel_id=1, replica_groups=mesh['job'=2,'row'=4,'slab'=2,'pair'=2] {'row'}, dimensions={1}, use_global_device_ids=true | all-gather | bytes 40960 | tf_op jit(solution)/shard_map/all_gather | solution.py:34
  21.6 0.0 copy-done.2
  21.6 8.0 %all_gather.11 = bf16[256,512]{1,0:T(8,128)(2,1)S(1)} all-gather(bf16[256,128]{1,0:T(8,128)(2,1)S(1)} %copy-done.2), channel_id=1, replica_groups=mesh['job'=2,'row'=4,'slab'=2,'pair'=2] {'slab','pair'}, dimensions={1}, use_global_device_ids=true | all-gather | bytes 327680 | tf_op jit(solution)/shard_map/all_gather | solution.py:32
  29.7 1.8 fusion.3
  31.5 0.0 reduce-scatter.2.cloned.1.call-update
  31.5 0.0 all-reduce.4.cloned.1.call-start
  31.6 18.7 %reduce-scatter.2.cloned.1.call-done = f32[128,256]{1,0:T(8,128)} async-done(((f32[512,256]{1,0:T(8,128)}), f32[128,256]{1,0:T(8,128)}) %reduce-scatter.2.cloned.1.call-update) | async-done | bytes 131088 | tf_op jit(solution)/shard_map/reduce_scatter | solution.py:36
  50.3 0.0 copy-start
  50.3 2.2 %fusion.25 = f32[256,256]{0,1:T(8,128)} fusion(f32[128,256]{1,0:T(8,128)} %reduce-scatter.2.cloned.1.call-done), kind=kOutput, calls=%fused_computation.45 | convolution fusion | flops 100663296 | bytes 393216 | tf_op jit(solution)/shard_map/dot_general | solution.py:42
  52.4 0.0 copy-done
  52.5 1.0 convolution_bitcast_fusion
  53.5 0.0 all-reduce.4.cloned.1.call-update
  53.5 91.5 %all-reduce.4.cloned.1.call-done = (f32[256,256]{0,1:T(8,128)}, f32[256,256]{0,1:T(8,128)}) async-done(((f32[256,256]{0,1:T(8,128)}, f32[256,256]{0,1:T(8,128)}), (f32[256,256]{0,1:T(8,128)}, f32[256,256]{0,1:T(8,128)})) %all-reduce.4.cloned.1.call-update) | async-done | bytes 524304 | tf_op jit(solution)/shard_map/psum | solution.py:44
  145.0 1.1 broadcast_multiply_fusion
  146.1 0.0 copy-start.1
  146.1 0.1 copy.6
  146.2 0.8 copy-done.1
  147.1 11.7 %cholesky.50 = f32[128,128]{1,0:T(8,128)S(1)} custom-call(f32[128,128]{1,0:T(8,128)S(1)} %cholesky.118), custom_call_target="Cholesky" | custom-call | tf_op jit(solution)/shard_map/jit(cholesky)/cholesky | solution.py:47
  158.8 0.6 compare_reduce_fusion.1
  159.5 9.8 %custom-call.11 = f32[1,128,128]{1,2,0:T(8,128)S(1)} custom-call(f32[1,128,128]{2,1,0:T(8,128)S(1)} %get-tuple-element.11), custom_call_target="InvertDiagBlocksLowerTriangular" | custom-call | tf_op jit(solution)/shard_map/jit(cholesky)/cholesky | solution.py:47
  169.3 0.2 constant_dynamic-update-slice_fusion.1
  169.5 0.3 convolution_subtract_fusion
  169.8 11.7 %cholesky.105 = f32[128,128]{1,0:T(8,128)S(1)} custom-call(f32[128,128]{1,0:T(8,128)S(1)} %convolution_subtract_fusion), custom_call_target="Cholesky" | custom-call | tf_op jit(solution)/shard_map/jit(cholesky)/cholesky | solution.py:47
  181.5 0.6 compare_reduce_fusion
  183.5 0.8 copy.8
  184.4 0.8 copy.7
  (8 shorter events, 0.2 us)
Async XLA Ops:
  7.2 6.0 %copy-start.3 = (bf16[32,128]{1,0:T(8,128)(2,1)S(1)}, bf16[32,128]{1,0:T(8,128)(2,1)}, u32[]{:S(2)}) copy-start(bf16[32,128]{1,0:T(8,128)(2,1)} %param.2) | copy-start | bytes 24580
  7.2 14.5 %copy-start.2 = (bf16[256,128]{1,0:T(8,128)(2,1)S(1)}, bf16[256,128]{1,0:T(8,128)(2,1)}, u32[]{:S(2)}) copy-start(bf16[256,128]{1,0:T(8,128)(2,1)} %param.3) | copy-start | bytes 196612
  7.2 43.1 %reduce-scatter.2.cloned.1.call-start = ((), (), s32[]{:S(2)}) async-start(), calls=%async_computation.1 | async-start | bytes 655360 | tf_op jit(solution)/shard_map/reduce_scatter | solution.py:36
  31.5 113.5 %all-reduce.4.cloned.1.call-start = ((), (), s32[]{:S(2)}) async-start(), calls=%async_computation.2 | async-start | bytes 1048576 | tf_op jit(solution)/shard_map/psum | solution.py:44
  50.3 2.2 %copy-start = (f32[128,256]{1,0:T(8,128)S(1)}, f32[128,256]{1,0:T(8,128)}, u32[]{:S(2)}) copy-start(f32[128,256]{1,0:T(8,128)} %reduce-scatter.2.cloned.1.call-done) | copy-start | bytes 393220
  146.1 1.0 copy-start.1
Sparse Core Ops, SparseCore 0:
  31.7 18.5 reduce-scatter.1
  54.3 90.6 all-reduce.3
where the time goes:
time: 195 us; the launch traced here: 192 us
  waiting for transfers between devices  110 us (56%)
  other arithmetic  35.8 us (18%)
  blocking collectives  22.4 us (11%)
  between operations  15.4 us (8%)
  matrix products  5.48 us (3%)
  local copies, waits for them, and re-layouts  2.65 us (1%)
    psum x1, waiting for transfers between devices, local(): lax.psum((gram_term, core_term), ('row', 'slab', 'pair'))  91.5 us
    another operation x7, other arithmetic, local(): upper_factor = jnp.linalg.cholesky(gram).T  34.6 us
    reduce_scatter x1, waiting for transfers between devices, local(): lax.psum_scatter(times_test(kernel_tile, block_tests), 'row', scatter_dim...  18.7 us
    all_gather x1, blocking collectives, local(): spread = lax.all_gather(points, 'row', axis=1, tiled=True)  8.45 us
    all_gather x1, blocking collectives, local(): lax.all_gather(test_matrix, ('slab', 'pair'), axis=1, tiled=True)  8.04 us
    all_gather x1, blocking collectives, local(): lax.all_gather(points, ('slab', 'pair'), axis=1, tiled=True)  5.89 us
  transfers between devices with their start and end apart: 2, of which 2 were waited for; matrix products, arithmetic and copies ran while one was open for 0% of the time, Pallas kernels for 0%

commit v1 on v0

v1 whole, which is shorter than its diff:
```python
import functools
import math

import jax
import jax.numpy as jnp
from jax import lax
from jax.experimental import pallas as pl
from jax.experimental.pallas import tpu as pltpu
from jax.sharding import PartitionSpec as P

MESH = pl.DeviceIdType.MESH


def loop(start, stop, body):
    if stop - start <= 8:
        for step in range(start, stop):
            body(step)
    else:
        lax.fori_loop(start, stop, lambda step, _: (body(step), 0)[1], 0)


def sketch_kernel(
    rows, slabs, pairs, points_ref, tests_ref, sketch_ref, core_ref, gram_ref,
    row_points, col_points, col_tests, part_out, part_in, plane, own_plane,
    terms, term_in, total,
    pt_sems, tt_sems, rp_sems, part_sems, plane_sems, term_sems, total_sems,
):
    block = slabs * pairs
    me_row = lax.axis_index("row")
    me = lax.axis_index("slab") * pairs + lax.axis_index("pair")
    feats, width = points_ref.shape
    tests = tests_ref.shape[0]
    chunk = tests // block

    def at_row(d):
        return lax.rem(me_row + d, rows)

    def at_block(d):
        return lax.rem(me + d, block)

    def block_id(index):
        return {"slab": index // pairs, "pair": lax.rem(index, pairs)}

    def lanes(index):
        return pl.ds(pl.multiple_of(index * width, width), width)

    def copy(src, dst, sems, to, sender, target):
        return pltpu.make_async_remote_copy(
            src_ref=src, dst_ref=dst, send_sem=sems.at[0, to], recv_sem=sems.at[1, sender],
            device_id=target, device_id_type=MESH,
        )

    barrier = pltpu.get_barrier_semaphore()
    loop(1, rows, lambda d: pl.semaphore_signal(
        barrier, inc=1, device_id={"row": at_row(d)}, device_id_type=MESH))
    loop(1, block, lambda d: pl.semaphore_signal(
        barrier, inc=1, device_id=block_id(at_block(d)), device_id_type=MESH))
    pl.semaphore_wait(barrier, rows + block - 2)

    def points_copy(to, sender):
        return copy(points_ref, col_points.at[:, lanes(sender)], pt_sems, to, sender, block_id(to))

    def tests_copy(to, sender):
        return copy(tests_ref, col_tests.at[:, lanes(sender)], tt_sems, to, sender, block_id(to))

    def row_copy(to, sender):
        return copy(points_ref, row_points.at[sender], rp_sems, to, sender, {"row": to})

    def part_copy(to, sender):
        return copy(part_out.at[to], part_in.at[sender], part_sems, to, sender, {"row": to})

    def plane_copy(to, sender):
        return copy(own_plane, plane.at[pl.ds(pl.multiple_of(sender * width, width), width), :],
                    plane_sems, to, sender, block_id(to))

    def term_copy(which, to, sender):
        return copy(terms.at[which, pl.ds(pl.multiple_of(me * chunk, chunk), chunk), :],
                    term_in.at[which, sender], term_sems.at[which], to, sender, {"row": to})

    def total_copy(which, to, sender):
        piece = pl.ds(pl.multiple_of(sender * chunk, chunk), chunk)
        return copy(total.at[which, piece, :], total.at[which, piece, :],
                    total_sems.at[which], to, sender, block_id(to))

    loop(1, block, lambda d: points_copy(at_block(d), me).start())
    loop(1, rows, lambda d: row_copy(at_row(d), me_row).start())
    loop(1, block, lambda d: tests_copy(at_block(d), me).start())
    row_points[me_row] = points_ref[...]
    col_points[:, lanes(me)] = points_ref[...]
    col_tests[:, lanes(me)] = tests_ref[...]

    length_scale = 0.35 * math.sqrt(feats)
    scale = 5.0 / (length_scale * length_scale)
    loop(1, block, lambda d: points_copy(at_block(d), at_block(d)).wait_recv())
    cols = col_points[...]
    cols32 = cols.astype(jnp.float32)
    col_squares = jnp.sum(cols32 * cols32, axis=0, keepdims=True) * scale

    def partial_sketch(row):
        picked = row_points[row].astype(jnp.float32).T
        squares = jnp.sum(picked * picked, axis=1, keepdims=True) * scale
        inner = jnp.dot(picked.astype(jnp.bfloat16), cols, preferred_element_type=jnp.float32)
        squared = jnp.maximum(squares + col_squares - (2.0 * scale) * inner, 1e-30)
        t = squared * lax.rsqrt(squared)
        tile = ((1.0 + t + squared * (1.0 / 3.0)) * jnp.exp(-t)).astype(jnp.bfloat16)
        return lax.dot_general(tile, col_tests[...], (((1,), (1,)), ((), ())),
                               preferred_element_type=jnp.float32)

    loop(1, block, lambda d: tests_copy(at_block(d), at_block(d)).wait_recv())

    def row_step(d):
        to = at_row(d)
        row_copy(to, to).wait_recv()
        part_out[to] = partial_sketch(to).astype(jnp.bfloat16)
        part_copy(to, me_row).start()

    loop(1, rows, row_step)
    sketch_ref[...] = partial_sketch(me_row)

    def part_step(d):
        part_copy(at_row(d), at_row(d)).wait_recv()
        sketch_ref[...] += part_in[at_row(d)].astype(jnp.float32)

    loop(1, rows, part_step)

    rounded = sketch_ref[...].astype(jnp.bfloat16)
    own_plane[...] = rounded
    loop(1, block, lambda d: plane_copy(at_block(d), me).start())
    plane[pl.ds(pl.multiple_of(me * width, width), width), :] = rounded
    loop(1, block, lambda d: plane_copy(at_block(d), at_block(d)).wait_recv())
    whole = plane[...]
    terms[0] = lax.dot_general(whole, whole, (((0,), (0,)), ((), ())),
                               preferred_element_type=jnp.float32)
    loop(1, rows, lambda d: term_copy(0, at_row(d), me_row).start())
    terms[1] = jnp.dot(col_tests[...], whole, preferred_element_type=jnp.float32)
    loop(1, rows, lambda d: term_copy(1, at_row(d), me_row).start())

    mine = pl.ds(pl.multiple_of(me * chunk, chunk), chunk)
    inverse = 1.0 / (width * rows * block)
    for which in (0, 1):
        term_in[which, me_row] = terms[which, mine, :]
        loop(1, rows, lambda d: term_copy(which, at_row(d), at_row(d)).wait_recv())
        total[which, mine, :] = jnp.sum(term_in[which], axis=0) * inverse
        loop(1, block, lambda d: total_copy(which, at_block(d), me).start())
    for which, out in ((0, gram_ref), (1, core_ref)):
        loop(1, block, lambda d: total_copy(which, at_block(d), at_block(d)).wait_recv())
        out[...] = total[which]

    def block_sent(d):
        to = at_block(d)
        for sent in (points_copy, tests_copy, plane_copy):
            sent(to, me).wait_send()
        for which in (0, 1):
            total_copy(which, to, me).wait_send()

    def row_sent(d):
        to = at_row(d)
        row_copy(to, me_row).wait_send()
        part_copy(to, me_row).wait_send()
        for which in (0, 1):
            term_copy(which, to, me_row).wait_send()

    loop(1, block, block_sent)
    loop(1, rows, row_sent)


def local(sizes, points, test_matrix):
    rows, slabs, pairs = sizes
    block = slabs * pairs
    feats, width = points.shape
    tests = test_matrix.shape[0]
    vmem = pl.BlockSpec(memory_space=pltpu.VMEM)
    square = jax.ShapeDtypeStruct((tests, tests), jnp.float32)
    sketch, core_matrix, gram = pl.pallas_call(
        functools.partial(sketch_kernel, rows, slabs, pairs),
        out_shape=(jax.ShapeDtypeStruct((width, tests), jnp.float32), square, square),
        in_specs=[vmem, vmem],
        out_specs=(vmem, vmem, vmem),
        scratch_shapes=[
            pltpu.VMEM((rows, feats, width), jnp.bfloat16),
            pltpu.VMEM((feats, block * width), jnp.bfloat16),
            pltpu.VMEM((tests, block * width), jnp.bfloat16),
            pltpu.VMEM((rows, width, tests), jnp.bfloat16),
            pltpu.VMEM((rows, width, tests), jnp.bfloat16),
            pltpu.VMEM((block * width, tests), jnp.bfloat16),
            pltpu.VMEM((width, tests), jnp.bfloat16),
            pltpu.VMEM((2, tests, tests), jnp.float32),
            pltpu.VMEM((2, rows, tests // block, tests), jnp.float32),
            pltpu.VMEM((2, tests, tests), jnp.float32),
            pltpu.SemaphoreType.DMA((2, block)),
            pltpu.SemaphoreType.DMA((2, block)),
            pltpu.SemaphoreType.DMA((2, rows)),
            pltpu.SemaphoreType.DMA((2, rows)),
            pltpu.SemaphoreType.DMA((2, block)),
            pltpu.SemaphoreType.DMA((2, 2, rows)),
            pltpu.SemaphoreType.DMA((2, 2, block)),
        ],
        compiler_params=pltpu.CompilerParams(
            collective_id=0, has_side_effects=True, vmem_limit_bytes=40 * 1024 * 1024
        ),
        name="sketch",
    )(points, test_matrix)
    upper_factor = jnp.linalg.cholesky(gram).T
    return (sketch, core_matrix, upper_factor)


def solution(mesh):
    sizes = tuple(mesh.shape[axis] for axis in ("row", "slab", "pair"))
    return jax.shard_map(
        functools.partial(local, sizes),
        mesh=mesh,
        in_specs=(P(None, ("job", "row", "slab", "pair")), P(None, ("row", "slab", "pair"))),
        out_specs=(P(("job", "row", "slab", "pair"), None), P("job", None), P("job", None)),
        check_vma=False,
    )
```

time: 195 us -> 78.5 us (0.40); the launches traced: 192 us -> 78.3 us
  waiting for transfers between devices: 110 us -> 0 us
  Pallas kernels: 0 us -> 37.9 us
  blocking collectives: 22.4 us -> 0 us
  between operations: 15.4 us -> 2 us
  matrix products: 5.48 us -> 0.47 us
    psum x1 -> x0, waiting for transfers between devices: 91.5 us -> none  [local(): lax.psum((gram_term, core_term), ('row', 'slab', 'pair'))]
    pallas_call x0 -> x1, Pallas kernels: none -> 37.9 us  [local(): pl.pallas_call(functools.partial(sketch_kernel, rows, slabs, pairs), out_...]
    all_gather x3 -> x0, blocking collectives: 22.4 us -> none  [the longest x1 8.45 us: local(): spread = lax.all_gather(points, 'row', axis=1, tiled=True)]
    reduce_scatter x1 -> x0, waiting for transfers between devices: 18.7 us -> none  [local(): lax.psum_scatter(times_test(kernel_tile, block_tests), 'row', scatter_dim...]
    dot_general x3 -> x0, matrix products: 5.01 us -> none  [the longest x1 2.16 us: local(): gram_term = jnp.dot(sketch.T, sketch, precision=lax.Precision.HIGHEST)]
    another operation x7 -> x6, other arithmetic: 34.6 us -> 34 us  [local(): upper_factor = jnp.linalg.cholesky(gram).T]
  transfers between devices with their start and end apart: 2 -> 0, of which waited for: 2 -> 0; matrix products, arithmetic and copies ran while one was open for 0% -> 0% of each run, Pallas kernels for 0% -> 0%
where the time goes in v1:
time: 78.5 us; the launch traced here: 78.3 us
  Pallas kernels  37.9 us (48%)
  other arithmetic  34 us (43%)
  local copies, waits for them, and re-layouts  3.88 us (5%)
  between operations  2 us (3%)
    pallas_call x1, Pallas kernels, local(): pl.pallas_call(functools.partial(sketch_kernel, rows, slabs, pairs), out_...  37.9 us
    another operation x6, other arithmetic, local(): upper_factor = jnp.linalg.cholesky(gram).T  34 us
    unnamed x7, local copies, waits for them, and re-layouts  3.72 us

profile of v1, /device:TPU:25, one launch (start us, length us, event | category | flops | bytes accessed | tf_op | source)
XLA Modules:
  0.0 78.3 jit_solution(9574137497666297417)
XLA Ops:
  0.6 0.0 copy-start
  0.6 0.8 %copy-done = bf16[256,128]{1,0:T(8,128)(2,1)S(1)} copy-done((bf16[256,128]{1,0:T(8,128)(2,1)S(1)}, bf16[256,128]{1,0:T(8,128)(2,1)}, u32[]{:S(2)}) %copy-start) | copy-done | bytes 65560
  1.5 0.0 copy-start.1
  1.5 0.7 copy-done.1
  2.2 37.9 %sketch.1 = (f32[128,256]{1,0:T(8,128)S(1)}, f32[256,256]{1,0:T(8,128)S(1)}, f32[256,256]{1,0:T(8,128)S(1)}) custom-call(bf16[32,128]{1,0:T(8,128)(2,1)S(1)} %copy-done.1, bf16[256,128]{1,0:T(8,128)(2,1)S(1)} %copy-done), custom_call_target="tpu_custom_call" | custom-call | tf_op jit(solution)/shard_map/sketch/pallas_call | solution.py:174
  40.1 0.1 copy.5
  40.3 11.7 %cholesky.50 = f32[128,128]{1,0:T(8,128)S(1)} custom-call(f32[128,128]{1,0:T(8,128)S(1)} %cholesky.118), custom_call_target="Cholesky" | custom-call | tf_op jit(solution)/shard_map/jit(cholesky)/cholesky | solution.py:203
  52.1 9.8 %custom-call.11 = f32[1,128,128]{1,2,0:T(8,128)S(1)} custom-call(f32[1,128,128]{2,1,0:T(8,128)S(1)} %get-tuple-element.15), custom_call_target="InvertDiagBlocksLowerTriangular" | custom-call | tf_op jit(solution)/shard_map/jit(cholesky)/cholesky | solution.py:203
  61.9 0.2 constant_dynamic-update-slice_fusion.1
  62.1 0.3 convolution_subtract_fusion
  62.4 11.7 %cholesky.105 = f32[128,128]{1,0:T(8,128)S(1)} custom-call(f32[128,128]{1,0:T(8,128)S(1)} %convolution_subtract_fusion), custom_call_target="Cholesky" | custom-call | tf_op jit(solution)/shard_map/jit(cholesky)/cholesky | solution.py:203
  74.1 0.6 compare_reduce_fusion
  76.1 0.8 %copy.6 = f32[256,256]{1,0:T(8,128)} copy(f32[256,256]{0,1:T(8,128)S(1)} %select_bitcast_fusion) | data formatting | bytes 524288
  76.9 0.7 copy.11
  77.6 0.7 copy.12
  (6 shorter events, 0.2 us)
Async XLA Ops:
  0.6 0.8 %copy-start = (bf16[256,128]{1,0:T(8,128)(2,1)S(1)}, bf16[256,128]{1,0:T(8,128)(2,1)}, u32[]{:S(2)}) copy-start(bf16[256,128]{1,0:T(8,128)(2,1)} %tests_ref.1) | copy-start | bytes 196612
  1.5 0.7 copy-start.1

commit v2 on v1

--- a/solution.py
+++ b/solution.py
@@ -162,6 +162,51 @@
 
     loop(1, block, block_sent)
     loop(1, rows, row_sent)
+
+
+def factor_kernel(gram_ref, upper_ref):
+    size = gram_ref.shape[0]
+    per, lanes = 8, 128
+    wide = size // lanes
+    group = lanes // per
+    panels = [
+        [gram_ref[q * per:(q + 1) * per, b * lanes:(b + 1) * lanes] for b in range(q // group, wide)]
+        for q in range(size // per)
+    ]
+    row_id = lax.broadcasted_iota(jnp.int32, (per, lanes), 0)
+    lane_id = lax.broadcasted_iota(jnp.int32, (per, lanes), 1)
+    for p in range(size // per):
+        first = p // group
+        lane = p * per - first * lanes
+        panel = panels[p]
+        columns = [jnp.broadcast_to(panel[0][:, lane + j:lane + j + 1], (per, lanes)) for j in range(per)]
+        small = [[columns[j][i:i + 1, :] for j in range(per)] for i in range(per)]
+        rows = [[piece[i:i + 1, :] for piece in panel] for i in range(per)]
+        for i in range(per):
+            inverse = lax.rsqrt(small[i][i])
+            for j in range(i + 1, per):
+                small[i][j] = small[i][j] * inverse
+            rows[i] = [piece * inverse for piece in rows[i]]
+            for j in range(i + 1, per):
+                for l in range(j, per):
+                    small[j][l] = small[j][l] - small[i][j] * small[i][l]
+                rows[j] = [a - small[i][j] * b for a, b in zip(rows[j], rows[i])]
+        done = [jnp.concatenate([rows[i][b] for i in range(per)], axis=0) for b in range(wide - first)]
+        done[0] = jnp.where(lane_id >= row_id + lane, done[0], 0.0)
+        for b in range(wide):
+            upper_ref[p * per:(p + 1) * per, b * lanes:(b + 1) * lanes] = (
+                done[b - first] if b >= first else jnp.zeros((per, lanes), jnp.float32))
+        turned = [piece.T for piece in done]
+        for q in range(p + 1, size // per):
+            start = q // group
+            offset = q * per - start * lanes
+            factors = turned[start - first][offset:offset + per, :]
+            for i in range(per):
+                factor = jnp.broadcast_to(factors[:, i:i + 1], (per, lanes))
+                panels[q] = [
+                    piece - factor * rows[i][start + b - first]
+                    for b, piece in enumerate(panels[q])
+                ]
 
 
 def local(sizes, points, test_matrix):
@@ -200,7 +245,11 @@
         ),
         name="sketch",
     )(points, test_matrix)
-    upper_factor = jnp.linalg.cholesky(gram).T
+    upper_factor = pl.pallas_call(
+        factor_kernel, out_shape=square, in_specs=[vmem], out_specs=vmem,
+        compiler_params=pltpu.CompilerParams(vmem_limit_bytes=40 * 1024 * 1024),
+        name="factor",
+    )(gram)
     return (sketch, core_matrix, upper_factor)
 
 

time: 78.5 us -> 56 us (0.71)
  other arithmetic: 34 us -> 0 us
  Pallas kernels: 37.9 us -> 52.2 us
  between operations: 2 us -> 0.65 us
  local copies, waits for them, and re-layouts: 3.88 us -> 2.89 us
    another operation x6 -> x0, other arithmetic: 34 us -> none  [local(): upper_factor = jnp.linalg.cholesky(gram).T]
    pallas_call x0 -> x1, Pallas kernels: none -> 14.3 us  [local(): pl.pallas_call(factor_kernel, out_shape=square, in_specs=[vmem], out_spec...]
    unnamed x7 -> x6, local copies, waits for them, and re-layouts: 3.72 us -> 2.89 us
where the time goes in v2:
time: 56 us; the launch traced here: 55.8 us
  Pallas kernels  52.2 us (93%)
  local copies, waits for them, and re-layouts  2.89 us (5%)
  between operations  0.65 us (1%)
    pallas_call x1, Pallas kernels, local(): pl.pallas_call(functools.partial(sketch_kernel, rows, slabs, pairs), out_...  37.9 us
    pallas_call x1, Pallas kernels, local(): pl.pallas_call(factor_kernel, out_shape=square, in_specs=[vmem], out_spec...  14.3 us
    unnamed x6, local copies, waits for them, and re-layouts  2.89 us

profile of v2, /device:TPU:25, one launch (start us, length us, event | category | flops | bytes accessed | tf_op | source)
XLA Modules:
  0.0 55.8 jit_solution(11373955159231347452)
XLA Ops:
  0.6 0.0 copy-start
  0.6 0.8 %copy-done = bf16[256,128]{1,0:T(8,128)(2,1)S(1)} copy-done((bf16[256,128]{1,0:T(8,128)(2,1)S(1)}, bf16[256,128]{1,0:T(8,128)(2,1)}, u32[]{:S(2)}) %copy-start) | copy-done | bytes 65560
  1.5 0.0 copy-start.1
  1.5 0.7 %copy-done.1 = bf16[32,128]{1,0:T(8,128)(2,1)S(1)} copy-done((bf16[32,128]{1,0:T(8,128)(2,1)S(1)}, bf16[32,128]{1,0:T(8,128)(2,1)}, u32[]{:S(2)}) %copy-start.1) | copy-done | bytes 8216
  2.2 37.9 %sketch.1 = (f32[128,256]{1,0:T(8,128)S(1)}, f32[256,256]{1,0:T(8,128)S(1)}, f32[256,256]{1,0:T(8,128)S(1)}) custom-call(bf16[32,128]{1,0:T(8,128)(2,1)S(1)} %copy-done.1, bf16[256,128]{1,0:T(8,128)(2,1)S(1)} %copy-done), custom_call_target="tpu_custom_call" | custom-call | tf_op jit(solution)/shard_map/sketch/pallas_call | solution.py:219
  40.1 14.3 %factor.1 = f32[256,256]{1,0:T(8,128)} custom-call(f32[256,256]{1,0:T(8,128)S(1)} %get-tuple-element.8.gram_ref), custom_call_target="tpu_custom_call" | custom-call | tf_op jit(solution)/shard_map/factor/pallas_call | solution.py:248
  54.4 0.7 %copy.7 = f32[128,256]{1,0:T(8,128)} copy(f32[128,256]{1,0:T(8,128)S(1)} %get-tuple-element.12) | data formatting | bytes 262144
  55.1 0.7 %copy.8 = f32[256,256]{1,0:T(8,128)} copy(f32[256,256]{1,0:T(8,128)S(1)} %get-tuple-element.13) | data formatting | bytes 524288
Async XLA Ops:
  0.6 0.8 %copy-start = (bf16[256,128]{1,0:T(8,128)(2,1)S(1)}, bf16[256,128]{1,0:T(8,128)(2,1)}, u32[]{:S(2)}) copy-start(bf16[256,128]{1,0:T(8,128)(2,1)} %tests_ref.1) | copy-start | bytes 196612
  1.5 0.7 %copy-start.1 = (bf16[32,128]{1,0:T(8,128)(2,1)S(1)}, bf16[32,128]{1,0:T(8,128)(2,1)}, u32[]{:S(2)}) copy-start(bf16[32,128]{1,0:T(8,128)(2,1)} %points_ref.1) | copy-start | bytes 24580

commit v3 on v1

--- a/solution.py
+++ b/solution.py
@@ -19,18 +19,68 @@
         lax.fori_loop(start, stop, lambda step, _: (body(step), 0)[1], 0)
 
 
+def factor(blocks, size, upper_ref, halfway):
+    per, lanes = 8, 128
+    wide = size // lanes
+    group = lanes // per
+    panels = [
+        [blocks[q // group, b][q % group * per:(q % group + 1) * per, :] for b in range(q // group, wide)]
+        for q in range(size // per)
+    ]
+    row_id = lax.broadcasted_iota(jnp.int32, (per, lanes), 0)
+    lane_id = lax.broadcasted_iota(jnp.int32, (per, lanes), 1)
+    for p in range(size // per):
+        if p == size // per // 2:
+            halfway()
+        first = p // group
+        lane = p * per - first * lanes
+        panel = panels[p]
+        columns = [jnp.broadcast_to(panel[0][:, lane + j:lane + j + 1], (per, lanes)) for j in range(per)]
+        small = [[columns[j][i:i + 1, :] for j in range(per)] for i in range(per)]
+        rows = [[piece[i:i + 1, :] for piece in panel] for i in range(per)]
+        for i in range(per):
+            inverse = lax.rsqrt(small[i][i])
+            for j in range(i + 1, per):
+                small[i][j] = small[i][j] * inverse
+            rows[i] = [piece * inverse for piece in rows[i]]
+            for j in range(i + 1, per):
+                for l in range(j, per):
+                    small[j][l] = small[j][l] - small[i][j] * small[i][l]
+                rows[j] = [a - small[i][j] * b for a, b in zip(rows[j], rows[i])]
+        done = [jnp.concatenate([rows[i][b] for i in range(per)], axis=0) for b in range(wide - first)]
+        done[0] = jnp.where(lane_id >= row_id + lane, done[0], 0.0)
+        for b in range(wide):
+            upper_ref[p * per:(p + 1) * per, b * lanes:(b + 1) * lanes] = (
+                done[b - first] if b >= first else jnp.zeros((per, lanes), jnp.float32))
+        turned = [piece.T for piece in done]
+        for q in range(p + 1, size // per):
+            start = q // group
+            offset = q * per - start * lanes
+            factors = turned[start - first][offset:offset + per, :]
+            for i in range(per):
+                factor = jnp.broadcast_to(factors[:, i:i + 1], (per, lanes))
+                panels[q] = [
+                    piece - factor * rows[i][start + b - first]
+                    for b, piece in enumerate(panels[q])
+                ]
+
+
 def sketch_kernel(
-    rows, slabs, pairs, points_ref, tests_ref, sketch_ref, core_ref, gram_ref,
+    rows, slabs, pairs, points_ref, tests_ref, sketch_ref, core_ref, upper_ref,
     row_points, col_points, col_tests, part_out, part_in, plane, own_plane,
-    terms, term_in, total,
-    pt_sems, tt_sems, rp_sems, part_sems, plane_sems, term_sems, total_sems,
+    gram_term, gram_in, gram_sum, core_term, core_in, core_sum,
+    pt_sems, tt_sems, rp_sems, part_sems, plane_sems, term_sems, total_sems, own_sems,
 ):
     block = slabs * pairs
     me_row = lax.axis_index("row")
     me = lax.axis_index("slab") * pairs + lax.axis_index("pair")
     feats, width = points_ref.shape
     tests = tests_ref.shape[0]
-    chunk = tests // block
+    terms, term_in, total = (gram_term, core_term), (gram_in, core_in), (gram_sum, core_sum)
+    mine = [
+        pl.ds(pl.multiple_of(me * (term.shape[0] // block), term.shape[0] // block), term.shape[0] // block)
+        for term in terms
+    ]
 
     def at_row(d):
         return lax.rem(me_row + d, rows)
@@ -50,11 +100,18 @@
             device_id=target, device_id_type=MESH,
         )
 
+    own_copies = [
+        pltpu.make_async_copy(points_ref, row_points.at[me_row], own_sems.at[0]),
+        pltpu.make_async_copy(points_ref, col_points.at[:, lanes(me)], own_sems.at[1]),
+        pltpu.make_async_copy(tests_ref, col_tests.at[:, lanes(me)], own_sems.at[2]),
+    ]
     barrier = pltpu.get_barrier_semaphore()
     loop(1, rows, lambda d: pl.semaphore_signal(
         barrier, inc=1, device_id={"row": at_row(d)}, device_id_type=MESH))
     loop(1, block, lambda d: pl.semaphore_signal(
         barrier, inc=1, device_id=block_id(at_block(d)), device_id_type=MESH))
+    for own in own_copies:
+        own.start()
     pl.semaphore_wait(barrier, rows + block - 2)
 
     def points_copy(to, sender):
@@ -74,20 +131,20 @@
                     plane_sems, to, sender, block_id(to))
 
     def term_copy(which, to, sender):
-        return copy(terms.at[which, pl.ds(pl.multiple_of(me * chunk, chunk), chunk), :],
-                    term_in.at[which, sender], term_sems.at[which], to, sender, {"row": to})
+        return copy(terms[which].at[mine[which], :],
+                    term_in[which].at[sender], term_sems.at[which], to, sender, {"row": to})
 
     def total_copy(which, to, sender):
+        chunk = terms[which].shape[0] // block
         piece = pl.ds(pl.multiple_of(sender * chunk, chunk), chunk)
-        return copy(total.at[which, piece, :], total.at[which, piece, :],
+        return copy(total[which].at[piece, :], total[which].at[piece, :],
                     total_sems.at[which], to, sender, block_id(to))
 
     loop(1, block, lambda d: points_copy(at_block(d), me).start())
     loop(1, rows, lambda d: row_copy(at_row(d), me_row).start())
     loop(1, block, lambda d: tests_copy(at_block(d), me).start())
-    row_points[me_row] = points_ref[...]
-    col_points[:, lanes(me)] = points_ref[...]
-    col_tests[:, lanes(me)] = tests_ref[...]
+    for own in own_copies:
+        own.wait()
 
     length_scale = 0.35 * math.sqrt(feats)
     scale = 5.0 / (length_scale * length_scale)
@@ -129,22 +186,34 @@
     plane[pl.ds(pl.multiple_of(me * width, width), width), :] = rounded
     loop(1, block, lambda d: plane_copy(at_block(d), at_block(d)).wait_recv())
     whole = plane[...]
-    terms[0] = lax.dot_general(whole, whole, (((0,), (0,)), ((), ())),
-                               preferred_element_type=jnp.float32)
+    lane = 128
+    wide = tests // lane
+    upper_blocks = [(a, b) for a in range(wide) for b in range(a, wide)]
+    for place, (a, b) in enumerate(upper_blocks):
+        gram_term[:, place * lane:(place + 1) * lane] = lax.dot_general(
+            whole[:, a * lane:(a + 1) * lane], whole[:, b * lane:(b + 1) * lane],
+            (((0,), (0,)), ((), ())), preferred_element_type=jnp.float32)
     loop(1, rows, lambda d: term_copy(0, at_row(d), me_row).start())
-    terms[1] = jnp.dot(col_tests[...], whole, preferred_element_type=jnp.float32)
+    core_term[...] = jnp.dot(col_tests[...], whole, preferred_element_type=jnp.float32)
     loop(1, rows, lambda d: term_copy(1, at_row(d), me_row).start())
-
-    mine = pl.ds(pl.multiple_of(me * chunk, chunk), chunk)
     inverse = 1.0 / (width * rows * block)
-    for which in (0, 1):
-        term_in[which, me_row] = terms[which, mine, :]
+
+    def sum_terms(which):
+        term_in[which][me_row] = terms[which][mine[which], :]
         loop(1, rows, lambda d: term_copy(which, at_row(d), at_row(d)).wait_recv())
-        total[which, mine, :] = jnp.sum(term_in[which], axis=0) * inverse
+        total[which][mine[which], :] = jnp.sum(term_in[which][...], axis=0) * inverse
         loop(1, block, lambda d: total_copy(which, at_block(d), me).start())
-    for which, out in ((0, gram_ref), (1, core_ref)):
+
+    def take_total(which):
         loop(1, block, lambda d: total_copy(which, at_block(d), at_block(d)).wait_recv())
-        out[...] = total[which]
+
+    sum_terms(0)
+    take_total(0)
+    blocks = {pair: gram_sum.at[:, place * lane:(place + 1) * lane]
+              for place, pair in enumerate(upper_blocks)}
+    factor(blocks, tests, upper_ref, lambda: sum_terms(1))
+    take_total(1)
+    core_ref[...] = core_sum[...]
 
     def block_sent(d):
         to = at_block(d)
@@ -170,11 +239,12 @@
     feats, width = points.shape
     tests = test_matrix.shape[0]
     vmem = pl.BlockSpec(memory_space=pltpu.VMEM)
+    packed = tests * (tests // 128 + 1) // 2
     square = jax.ShapeDtypeStruct((tests, tests), jnp.float32)
-    sketch, core_matrix, gram = pl.pallas_call(
+    sketch, core_matrix, upper_factor = pl.pallas_call(
         functools.partial(sketch_kernel, rows, slabs, pairs),
         out_shape=(jax.ShapeDtypeStruct((width, tests), jnp.float32), square, square),
-        in_specs=[vmem, vmem],
+        in_specs=[pl.BlockSpec(memory_space=pl.ANY)] * 2,
         out_specs=(vmem, vmem, vmem),
         scratch_shapes=[
             pltpu.VMEM((rows, feats, width), jnp.bfloat16),
@@ -184,9 +254,12 @@
             pltpu.VMEM((rows, width, tests), jnp.bfloat16),
             pltpu.VMEM((block * width, tests), jnp.bfloat16),
             pltpu.VMEM((width, tests), jnp.bfloat16),
-            pltpu.VMEM((2, tests, tests), jnp.float32),
-            pltpu.VMEM((2, rows, tests // block, tests), jnp.float32),
-            pltpu.VMEM((2, tests, tests), jnp.float32),
+            pltpu.VMEM((128, packed), jnp.float32),
+            pltpu.VMEM((rows, 128 // block, packed), jnp.float32),
+            pltpu.VMEM((128, packed), jnp.float32),
+            pltpu.VMEM((tests, tests), jnp.float32),
+            pltpu.VMEM((rows, tests // block, tests), jnp.float32),
+            pltpu.VMEM((tests, tests), jnp.float32),
             pltpu.SemaphoreType.DMA((2, block)),
             pltpu.SemaphoreType.DMA((2, block)),
             pltpu.SemaphoreType.DMA((2, rows)),
@@ -194,13 +267,13 @@
             pltpu.SemaphoreType.DMA((2, block)),
             pltpu.SemaphoreType.DMA((2, 2, rows)),
             pltpu.SemaphoreType.DMA((2, 2, block)),
+            pltpu.SemaphoreType.DMA((3,)),
         ],
         compiler_params=pltpu.CompilerParams(
-            collective_id=0, has_side_effects=True, vmem_limit_bytes=40 * 1024 * 1024
+            collective_id=0, has_side_effects=True, vmem_limit_bytes=60 * 1024 * 1024
         ),
         name="sketch",
     )(points, test_matrix)
-    upper_factor = jnp.linalg.cholesky(gram).T
     return (sketch, core_matrix, upper_factor)
 
 

time: 78.5 us -> 51.9 us (0.66)
  other arithmetic: 34 us -> 0 us
  Pallas kernels: 37.9 us -> 47.7 us
  between operations: 2 us -> 0.65 us
    another operation x6 -> x0, other arithmetic: 34 us -> none  [local(): upper_factor = jnp.linalg.cholesky(gram).T]
    pallas_call x1, Pallas kernels: 37.9 us -> 47.7 us  [local(): pl.pallas_call(functools.partial(sketch_kernel, rows, slabs, pairs), out_...]
where the time goes in v3:
time: 51.9 us; the launch traced here: 51.7 us
  Pallas kernels  47.7 us (92%)
  local copies, waits for them, and re-layouts  3.36 us (6%)
  between operations  0.65 us (1%)
    pallas_call x1, Pallas kernels, local(): pl.pallas_call(functools.partial(sketch_kernel, rows, slabs, pairs), out_...  47.7 us
    unnamed x7, local copies, waits for them, and re-layouts  3.36 us

profile of v3, /device:TPU:25, one launch (start us, length us, event | category | flops | bytes accessed | tf_op | source)
XLA Modules:
  0.0 51.7 jit_solution(14407434293119545246)
XLA Ops:
  0.6 47.7 %sketch.1 = (f32[128,256]{1,0:T(8,128)}, f32[256,256]{1,0:T(8,128)}, f32[256,256]{1,0:T(8,128)}) custom-call(bf16[32,128]{1,0:T(8,128)(2,1)} %points_ref.1, bf16[256,128]{1,0:T(8,128)(2,1)} %tests_ref.1), custom_call_target="tpu_custom_call" | custom-call | tf_op jit(solution)/shard_map/sketch/pallas_call | solution.py:244
  48.3 0.0 copy-start.1
  48.3 1.6 %copy.8 = f32[128,256]{1,0:T(8,128)} copy(f32[128,256]{1,0:T(8,128)} %get-tuple-element.6) | data formatting | bytes 262144
  49.9 0.0 copy-done.1
  49.9 0.0 copy-start
  49.9 0.7 %copy.9 = f32[256,256]{1,0:T(8,128)} copy(f32[256,256]{1,0:T(8,128)S(1)} %copy-done.1) | data formatting | bytes 524288
  50.6 0.3 copy-done
  51.0 0.7 %copy.10 = f32[256,256]{1,0:T(8,128)} copy(f32[256,256]{1,0:T(8,128)S(1)} %copy-done) | data formatting | bytes 524288
Async XLA Ops:
  48.3 1.6 %copy-start.1 = (f32[256,256]{1,0:T(8,128)S(1)}, f32[256,256]{1,0:T(8,128)}, u32[]{:S(2)}) copy-start(f32[256,256]{1,0:T(8,128)} %get-tuple-element.7) | copy-start | bytes 786436
  49.9 1.0 %copy-start = (f32[256,256]{1,0:T(8,128)S(1)}, f32[256,256]{1,0:T(8,128)}, u32[]{:S(2)}) copy-start(f32[256,256]{1,0:T(8,128)} %get-tuple-element.8) | copy-start | bytes 786436

commit v4 on v3

--- a/solution.py
+++ b/solution.py
@@ -67,7 +67,7 @@
 
 def sketch_kernel(
     rows, slabs, pairs, points_ref, tests_ref, sketch_ref, core_ref, upper_ref,
-    row_points, col_points, col_tests, part_out, part_in, plane, own_plane,
+    row_points, col_points, col_tests, tiles, part_out, part_in, plane, own_plane,
     gram_term, gram_in, gram_sum, core_term, core_in, core_sum,
     pt_sems, tt_sems, rp_sems, part_sems, plane_sems, term_sems, total_sems, own_sems,
 ):
@@ -153,21 +153,28 @@
     cols32 = cols.astype(jnp.float32)
     col_squares = jnp.sum(cols32 * cols32, axis=0, keepdims=True) * scale
 
-    def partial_sketch(row):
+    def make_tile(row):
         picked = row_points[row].astype(jnp.float32).T
         squares = jnp.sum(picked * picked, axis=1, keepdims=True) * scale
         inner = jnp.dot(picked.astype(jnp.bfloat16), cols, preferred_element_type=jnp.float32)
         squared = jnp.maximum(squares + col_squares - (2.0 * scale) * inner, 1e-30)
         t = squared * lax.rsqrt(squared)
-        tile = ((1.0 + t + squared * (1.0 / 3.0)) * jnp.exp(-t)).astype(jnp.bfloat16)
-        return lax.dot_general(tile, col_tests[...], (((1,), (1,)), ((), ())),
+        tiles[row] = ((1.0 + t + squared * (1.0 / 3.0)) * jnp.exp(-t)).astype(jnp.bfloat16)
+
+    def partial_sketch(row):
+        return lax.dot_general(tiles[row], col_tests[...], (((1,), (1,)), ((), ())),
                                preferred_element_type=jnp.float32)
 
+    def tile_step(d):
+        row_copy(at_row(d), at_row(d)).wait_recv()
+        make_tile(at_row(d))
+
+    make_tile(me_row)
+    loop(1, rows, tile_step)
     loop(1, block, lambda d: tests_copy(at_block(d), at_block(d)).wait_recv())
 
     def row_step(d):
         to = at_row(d)
-        row_copy(to, to).wait_recv()
         part_out[to] = partial_sketch(to).astype(jnp.bfloat16)
         part_copy(to, me_row).start()
 
@@ -195,7 +202,6 @@
             (((0,), (0,)), ((), ())), preferred_element_type=jnp.float32)
     loop(1, rows, lambda d: term_copy(0, at_row(d), me_row).start())
     core_term[...] = jnp.dot(col_tests[...], whole, preferred_element_type=jnp.float32)
-    loop(1, rows, lambda d: term_copy(1, at_row(d), me_row).start())
     inverse = 1.0 / (width * rows * block)
 
     def sum_terms(which):
@@ -208,6 +214,7 @@
         loop(1, block, lambda d: total_copy(which, at_block(d), at_block(d)).wait_recv())
 
     sum_terms(0)
+    loop(1, rows, lambda d: term_copy(1, at_row(d), me_row).start())
     take_total(0)
     blocks = {pair: gram_sum.at[:, place * lane:(place + 1) * lane]
               for place, pair in enumerate(upper_blocks)}
@@ -233,23 +240,38 @@
     loop(1, rows, row_sent)
 
 
+def write_out(sketch_ref, core_ref, upper_ref, sketch_out, core_out, upper_out, sems):
+    copies = [
+        pltpu.make_async_copy(source, target, sems.at[place])
+        for place, (source, target) in enumerate(
+            ((sketch_ref, sketch_out), (core_ref, core_out), (upper_ref, upper_out)))
+    ]
+    for one in copies:
+        one.start()
+    for one in copies:
+        one.wait()
+
+
 def local(sizes, points, test_matrix):
     rows, slabs, pairs = sizes
     block = slabs * pairs
     feats, width = points.shape
     tests = test_matrix.shape[0]
     vmem = pl.BlockSpec(memory_space=pltpu.VMEM)
+    hbm = pl.BlockSpec(memory_space=pl.ANY)
     packed = tests * (tests // 128 + 1) // 2
     square = jax.ShapeDtypeStruct((tests, tests), jnp.float32)
-    sketch, core_matrix, upper_factor = pl.pallas_call(
+    shapes = (jax.ShapeDtypeStruct((width, tests), jnp.float32), square, square)
+    results = pl.pallas_call(
         functools.partial(sketch_kernel, rows, slabs, pairs),
-        out_shape=(jax.ShapeDtypeStruct((width, tests), jnp.float32), square, square),
-        in_specs=[pl.BlockSpec(memory_space=pl.ANY)] * 2,
+        out_shape=shapes,
+        in_specs=[hbm, hbm],
         out_specs=(vmem, vmem, vmem),
         scratch_shapes=[
             pltpu.VMEM((rows, feats, width), jnp.bfloat16),
             pltpu.VMEM((feats, block * width), jnp.bfloat16),
             pltpu.VMEM((tests, block * width), jnp.bfloat16),
+            pltpu.VMEM((rows, width, block * width), jnp.bfloat16),
             pltpu.VMEM((rows, width, tests), jnp.bfloat16),
             pltpu.VMEM((rows, width, tests), jnp.bfloat16),
             pltpu.VMEM((block * width, tests), jnp.bfloat16),
@@ -274,7 +296,14 @@
         ),
         name="sketch",
     )(points, test_matrix)
-    return (sketch, core_matrix, upper_factor)
+    return pl.pallas_call(
+        write_out,
+        out_shape=shapes,
+        in_specs=[hbm] * 3,
+        out_specs=(hbm, hbm, hbm),
+        scratch_shapes=[pltpu.SemaphoreType.DMA((3,))],
+        name="write_out",
+    )(*results)
 
 
 def solution(mesh):

time: 51.9 us -> 67.1 us (1.29)
  Pallas kernels: 47.7 us -> 65.7 us
  local copies, waits for them, and re-layouts: 3.36 us -> 0 us
    pallas_call x0 -> x1, Pallas kernels: none -> 21 us  [local(): pl.pallas_call(write_out, out_shape=shapes, in_specs=[hbm] * 3, out_specs...]
    unnamed x7 -> x0, local copies, waits for them, and re-layouts: 3.36 us -> none
    pallas_call x1, Pallas kernels: 47.7 us -> 44.8 us  [local(): pl.pallas_call(functools.partial(sketch_kernel, rows, slabs, pairs), out_...]
where the time goes in v4:
time: 67.1 us; the launch traced here: 66.4 us
  Pallas kernels  65.7 us (98%)
    pallas_call x1, Pallas kernels, local(): pl.pallas_call(functools.partial(sketch_kernel, rows, slabs, pairs), out_...  44.8 us
    pallas_call x1, Pallas kernels, local(): pl.pallas_call(write_out, out_shape=shapes, in_specs=[hbm] * 3, out_specs...  21 us

profile of v4, /device:TPU:25, one launch (start us, length us, event | category | flops | bytes accessed | tf_op | source)
XLA Modules:
  0.0 66.4 jit_solution(10161788419518218113)
XLA Ops:
  0.6 44.8 %sketch.1 = (f32[128,256]{1,0:T(8,128)}, f32[256,256]{1,0:T(8,128)}, f32[256,256]{1,0:T(8,128)}) custom-call(bf16[32,128]{1,0:T(8,128)(2,1)} %points_ref.1, bf16[256,128]{1,0:T(8,128)(2,1)} %tests_ref.1), custom_call_target="tpu_custom_call" | custom-call | tf_op jit(solution)/shard_map/sketch/pallas_call | solution.py:265
  45.4 21.0 %write_out.1 = (f32[128,256]{1,0:T(8,128)}, f32[256,256]{1,0:T(8,128)}, f32[256,256]{1,0:T(8,128)}) custom-call(f32[128,256]{1,0:T(8,128)} %get-tuple-element.6.sketch_ref, f32[256,256]{1,0:T(8,128)} %get-tuple-element.7.core_ref, f32[256,256]{1,0:T(8,128)} %get-tuple-element.8.upper_ref), custom_call_target="tpu_custom_call" | custom-call | tf_op jit(solution)/shard_map/write_out/pallas_call | solution.py:299
